TPU v7x, 32 devices: a whole 2x2x4 slice. The times are simulated.
32 devices in a mesh: dp: 16 (over z, y, x), mp: 2 (over core).
Axes of the slice: x: 2, y: 2, z: 4, core: 2. Of those that a mesh axis runs over, the one named last changes fastest.
Arguments:
- text: bfloat16 [192, 61, 768], P('dp'), may hold values from -6 to 6
- patches: bfloat16 [192, 145, 1024], P(('dp', 'mp')), may hold values from -6 to 6
- cotangent: bfloat16 [192, 61, 768], P('dp'), may hold values from -6 to 6
- region_counts: int32 [192], P('dp'), may hold values from 0 to 6, as said below
- phrase_starts: int32 [192, 6], P('dp'), may hold values from 0 to 60, as said below
- phrase_lengths: int32 [192, 6], P('dp'), may hold values from 1 to 8
- box_patches: int32 [192, 6, 16], P('dp'), may hold values from 0 to 144
- query_weight: bfloat16 [768, 768], P('dp', 'mp'), may hold values from -0.21875 to 0.21875
- key_weight: bfloat16 [768, 768], P('dp', 'mp'), may hold values from -0.21875 to 0.21875
- value_weight: bfloat16 [768, 768], P('dp', 'mp'), may hold values from -0.21875 to 0.21875
- attn_out_weight: bfloat16 [768, 768], P('mp', 'dp'), may hold values from -1.75 to 1.75
- cross_query_weight: bfloat16 [768, 768], P('dp', 'mp'), may hold values from -0.21875 to 0.21875
- cross_key_weight: bfloat16 [768, 768], P('dp', 'mp'), may hold values from -0.21875 to 0.21875
- cross_value_weight: bfloat16 [768, 768], P('dp', 'mp'), may hold values from -0.21875 to 0.21875
- cross_out_weight: bfloat16 [768, 768], P('mp', 'dp'), may hold values from -2.5 to 2.5
- image_weight: bfloat16 [1024, 768], P('dp'), may hold values from -0.1875 to 0.1875
- ffn_in_weight: bfloat16 [768, 3072], P('dp', 'mp'), may hold values from -0.21875 to 0.21875
- ffn_out_weight: bfloat16 [3072, 768], P('mp', 'dp'), may hold values from -0.109375 to 0.109375
- text_embed_weight: bfloat16 [768, 256], P('dp'), may hold values from -0.21875 to 0.21875
- image_embed_weight: bfloat16 [768, 256], P('dp'), may hold values from -0.21875 to 0.21875
- ln_attn_gain: bfloat16 [768], P('dp'), may hold values from 0.5 to 1.5
- ln_attn_bias: bfloat16 [768], P('dp'), may hold values from -1.1953125 to 1.1953125
- ln_cross_gain: bfloat16 [768], P('dp'), may hold values from 0.5 to 1.5
- ln_cross_bias: bfloat16 [768], P('dp'), may hold values from -1.1953125 to 1.1953125
- ln_ffn_gain: bfloat16 [768], P('dp'), may hold values from 0.5 to 1.5
- ln_ffn_bias: bfloat16 [768], P('dp'), may hold values from -1.1953125 to 1.1953125
Outputs:
- joined: bfloat16 [192, 61, 768], P('dp')
- text_grad: float32 [192, 61, 768], P('dp')
- patch_grad: float32 [192, 145, 1024], P(('dp', 'mp'))
- grad_query: float32 [768, 768], P('dp', 'mp')
- grad_key: float32 [768, 768], P('dp', 'mp')
- grad_value: float32 [768, 768], P('dp', 'mp')
- grad_attn_out: float32 [768, 768], P('mp', 'dp')
- grad_cross_query: float32 [768, 768], P('dp', 'mp')
- grad_cross_key: float32 [768, 768], P('dp', 'mp')
- grad_cross_value: float32 [768, 768], P('dp', 'mp')
- grad_cross_out: float32 [768, 768], P('mp', 'dp')
- grad_image: float32 [1024, 768], P('dp')
- grad_ffn_in: float32 [768, 3072], P('dp', 'mp')
- grad_ffn_out: float32 [3072, 768], P('mp', 'dp')
- grad_text_embed: float32 [768, 256], P('dp')
- grad_image_embed: float32 [768, 256], P('dp')
- grad_attn_gain: float32 [768], P('dp')
- grad_attn_bias: float32 [768], P('dp')
- grad_cross_gain: float32 [768], P('dp')
- grad_cross_bias: float32 [768], P('dp')
- grad_ffn_gain: float32 [768], P('dp')
- grad_ffn_bias: float32 [768], P('dp')
Inputs may be any that keep to these rules, and one draw needn't show every extreme that they name: `region_counts`: some image has 6 boxed phrases and some has none. `phrase_starts`: each box's phrase ends within its caption: start + length <= 61.
All inputs are finite; a program needn't handle non-finite values.
Results may differ from a plain program's by a relative error of at most 0.022.
Values may be sent and summed in bfloat16 or wider, within the bound.
A program may use at most 192 MiB of HBM per device.

v0:
```python
import math

import jax
import jax.numpy as jnp
from jax import lax
from jax.sharding import PartitionSpec as P

HEAD_DIM = 64


EPS = 1e-06
TEMP_INVERSE = 20.0
GRAD_SCALE = 10.0
HIGHEST = lax.Precision.HIGHEST


def in_blocks(x, dim, count):
    dims = x.shape
    parts = x.reshape(*dims[:dim], count, dims[dim] // count, *dims[dim + 1 :])
    return jnp.moveaxis(parts, dim, 0)


def sum_at_owner(x, axis, dim):
    parts = in_blocks(x, dim, lax.axis_size(axis))
    arrived = lax.all_to_all(parts, axis, split_axis=0, concat_axis=0, tiled=True)
    return arrived.astype(jnp.float32).sum(axis=0)


def in_one_piece(arrays, axis, dim, along):
    widths = [a.shape[along] for a in arrays]
    both = jnp.concatenate(arrays, axis=along)
    result = sum_at_owner(both, axis, dim)
    return tuple(jnp.split(result, [sum(widths[:k]) for k in range(1, len(widths))], axis=along))


def side_by_side(arrays, axis, dim, along):
    columns = [a.reshape(*a.shape[:along], -1) for a in arrays]
    both = jnp.concatenate(columns, axis=along)
    result, at, outs = (sum_at_owner(both, axis, dim), 0, [])
    for a, column in zip(arrays, columns):
        slab = result[..., at : at + column.shape[along]]
        outs.append(slab.reshape(*slab.shape[:along], *a.shape[along:]))
        at += column.shape[along]
    return tuple(outs)


def matmul(left, right):
    return jnp.dot(left, right, preferred_element_type=jnp.float32)


def contract_rows(left, right):
    return lax.dot_general(
        left, right, (((0,), (0,)), ((), ())), preferred_element_type=jnp.float32
    )


def contract_cols(left, right):
    return lax.dot_general(
        left, right, (((1,), (1,)), ((), ())), preferred_element_type=jnp.float32
    )


def layer_norm(inputs, gain, shift):
    centred = inputs - jnp.mean(inputs, -1, keepdims=True)
    inv_std = lax.rsqrt(jnp.mean(centred * centred, -1, keepdims=True) + EPS)
    normed = centred * inv_std
    return (normed * gain + shift, normed, inv_std)


def norm_back(upstream, normed, inv_std, gain):
    scaled = upstream * gain
    inner_mean = jnp.mean(scaled * normed, -1, keepdims=True)
    result = inv_std * (scaled - jnp.mean(scaled, -1, keepdims=True) - normed * inner_mean)
    return (result, jnp.sum(upstream * normed, 0), jnp.sum(upstream, 0))


def split_heads(flat, pair_count):
    return flat.reshape(pair_count, -1, flat.shape[-1] // HEAD_DIM, HEAD_DIM)


def attend(queries, key_heads, value_heads):
    factor = 1.0 / math.sqrt(HEAD_DIM)
    scores = (
        jnp.einsum("pqhd,pkhd->phqk", queries, key_heads, preferred_element_type=jnp.float32)
        * factor
    )
    row_max = jnp.max(scores, -1, keepdims=True)
    expd = jnp.exp(scores - row_max)
    row_sum = jnp.sum(expd, -1, keepdims=True)
    probs = (expd / row_sum).astype(jnp.bfloat16)
    mixed = jnp.einsum("phqk,pkhd->pqhd", probs, value_heads, preferred_element_type=jnp.float32)
    flat_rows = queries.shape[0] * queries.shape[1]
    return (mixed.astype(jnp.bfloat16).reshape(flat_rows, -1), row_max + jnp.log(row_sum))


def attend_back(queries, key_heads, value_heads, log_total, upstream):
    factor = 1.0 / math.sqrt(HEAD_DIM)
    scores = (
        jnp.einsum("pqhd,pkhd->phqk", queries, key_heads, preferred_element_type=jnp.float32)
        * factor
    )
    probs = jnp.exp(scores - log_total)
    dprobs = jnp.einsum(
        "pqhd,pkhd->phqk", upstream, value_heads, preferred_element_type=jnp.float32
    )
    dscores = (probs * (dprobs - jnp.sum(dprobs * probs, -1, keepdims=True))).astype(jnp.bfloat16)
    dqueries = (
        jnp.einsum("phqk,pkhd->pqhd", dscores, key_heads, preferred_element_type=jnp.float32)
        * factor
    )
    dkeys = (
        jnp.einsum("phqk,pqhd->pkhd", dscores, queries, preferred_element_type=jnp.float32) * factor
    )
    dvalues = jnp.einsum(
        "phqk,pqhd->pkhd", probs.astype(jnp.bfloat16), upstream, preferred_element_type=jnp.float32
    )
    return tuple(
        (
            tensor.astype(jnp.bfloat16).reshape(-1, tensor.shape[2] * tensor.shape[3])
            for tensor in (dqueries, dkeys, dvalues)
        )
    )


def unit_back(raw, inv_norm, upstream):
    cubed = inv_norm * inv_norm * inv_norm
    return inv_norm * upstream - raw * cubed * jnp.sum(raw * upstream, -1, keepdims=True)


def branch_sum(partial_sum):
    return lax.psum(partial_sum, "mp")


def stream_sum(partial_sum):
    return lax.psum(partial_sum.astype(jnp.bfloat16), "mp").astype(jnp.float32)


def gather_weights(
    query_w,
    key_w,
    value_w,
    attn_out_w,
    cross_query_w,
    cross_key_w,
    cross_value_w,
    cross_out_w,
    image_w,
    ffn_in_w,
    ffn_out_w,
    text_embed_w,
    image_embed_w,
    gain_one,
    bias_one,
    gain_two,
    bias_two,
    gain_three,
    bias_three,
):
    return (
        lax.all_gather(query_w, "dp", axis=0, tiled=True),
        lax.all_gather(key_w, "dp", axis=0, tiled=True),
        lax.all_gather(value_w, "dp", axis=0, tiled=True),
        lax.all_gather(attn_out_w, "dp", axis=1, tiled=True),
        lax.all_gather(cross_query_w, "dp", axis=0, tiled=True),
        lax.all_gather(cross_key_w, "dp", axis=0, tiled=True),
        lax.all_gather(cross_value_w, "dp", axis=0, tiled=True),
        lax.all_gather(cross_out_w, "dp", axis=1, tiled=True),
        lax.all_gather(image_w, "dp", axis=0, tiled=True),
        lax.all_gather(ffn_in_w, "dp", axis=0, tiled=True),
        lax.all_gather(ffn_out_w, "dp", axis=1, tiled=True),
        lax.all_gather(text_embed_w, "dp", axis=0, tiled=True),
        lax.all_gather(image_embed_w, "dp", axis=0, tiled=True),
        lax.all_gather(gain_one, "dp", axis=0, tiled=True),
        lax.all_gather(bias_one, "dp", axis=0, tiled=True),
        lax.all_gather(gain_two, "dp", axis=0, tiled=True),
        lax.all_gather(bias_two, "dp", axis=0, tiled=True),
        lax.all_gather(gain_three, "dp", axis=0, tiled=True),
        lax.all_gather(bias_three, "dp", axis=0, tiled=True),
    )


def layer_forward(text, patches, weights):
    (
        query_w,
        key_w,
        value_w,
        attn_out_w,
        cross_query_w,
        cross_key_w,
        cross_value_w,
        cross_out_w,
        image_w,
        ffn_in_w,
        ffn_out_w,
        text_embed_w,
        image_embed_w,
        gain_one,
        bias_one,
        gain_two,
        bias_two,
        gain_three,
        bias_three,
    ) = weights
    pair_count, length, model_width = text.shape
    text_rows = text.reshape(pair_count * length, model_width)
    half_pairs = patches.shape[0]
    patch_rows = patches.reshape(half_pairs * patches.shape[1], patches.shape[2])
    image_part = (
        matmul(patch_rows, image_w).astype(jnp.bfloat16).reshape(half_pairs, -1, model_width)
    )
    image_feats = lax.all_gather(image_part, "mp", axis=0, tiled=True)
    image_rows = image_feats.reshape(-1, model_width)
    queries = split_heads(matmul(text_rows, query_w).astype(jnp.bfloat16), pair_count)
    key_heads = split_heads(matmul(text_rows, key_w).astype(jnp.bfloat16), pair_count)
    value_heads = split_heads(matmul(text_rows, value_w).astype(jnp.bfloat16), pair_count)
    self_mixed, self_total = attend(queries, key_heads, value_heads)
    first = text_rows.astype(jnp.float32) + branch_sum(matmul(self_mixed, attn_out_w))
    hidden_one, normed_one, inv_one = layer_norm(
        first, gain_one.astype(jnp.float32), bias_one.astype(jnp.float32)
    )
    low_one = hidden_one.astype(jnp.bfloat16)
    cross_queries = split_heads(matmul(low_one, cross_query_w).astype(jnp.bfloat16), pair_count)
    cross_keys = split_heads(matmul(image_rows, cross_key_w).astype(jnp.bfloat16), pair_count)
    cross_values = split_heads(matmul(image_rows, cross_value_w).astype(jnp.bfloat16), pair_count)
    cross_mixed, cross_total = attend(cross_queries, cross_keys, cross_values)
    second = hidden_one + branch_sum(matmul(cross_mixed, cross_out_w))
    hidden_two, normed_two, inv_two = layer_norm(
        second, gain_two.astype(jnp.float32), bias_two.astype(jnp.float32)
    )
    low_two = hidden_two.astype(jnp.bfloat16)
    inner = matmul(low_two, ffn_in_w)
    active = jax.nn.gelu(inner, approximate=False).astype(jnp.bfloat16)
    third = hidden_two + branch_sum(matmul(active, ffn_out_w))
    output, normed_three, inv_three = layer_norm(
        third, gain_three.astype(jnp.float32), bias_three.astype(jnp.float32)
    )
    return {
        "text_rows": text_rows,
        "image": image_feats,
        "image_rows": image_rows,
        "queries": queries,
        "key_heads": key_heads,
        "value_heads": value_heads,
        "self_mixed": self_mixed,
        "self_total": self_total,
        "normed_one": normed_one,
        "inv_one": inv_one,
        "low_one": low_one,
        "cross_queries": cross_queries,
        "cross_keys": cross_keys,
        "cross_values": cross_values,
        "cross_mixed": cross_mixed,
        "cross_total": cross_total,
        "normed_two": normed_two,
        "inv_two": inv_two,
        "low_two": low_two,
        "inner": inner,
        "active": active,
        "normed_three": normed_three,
        "inv_three": inv_three,
        "output": output,
    }


def body(
    text,
    patches,
    cotangent,
    region_counts,
    phrase_starts,
    phrase_lengths,
    box_patches,
    query_weight,
    key_weight,
    value_weight,
    attn_out_weight,
    cross_query_weight,
    cross_key_weight,
    cross_value_weight,
    cross_out_weight,
    image_weight,
    ffn_in_weight,
    ffn_out_weight,
    text_embed_weight,
    image_embed_weight,
    ln_attn_gain,
    ln_attn_bias,
    ln_cross_gain,
    ln_cross_bias,
    ln_ffn_gain,
    ln_ffn_bias,
):
    shards = (
        query_weight,
        key_weight,
        value_weight,
        attn_out_weight,
        cross_query_weight,
        cross_key_weight,
        cross_value_weight,
        cross_out_weight,
        image_weight,
        ffn_in_weight,
        ffn_out_weight,
        text_embed_weight,
        image_embed_weight,
        ln_attn_gain,
        ln_attn_bias,
        ln_cross_gain,
        ln_cross_bias,
        ln_ffn_gain,
        ln_ffn_bias,
    )
    weights = gather_weights(*shards)
    saved = layer_forward(text, patches, weights)
    pair_count, length, model_width = text.shape
    half_pairs, patch_count, _ = patches.shape
    text32 = text.astype(jnp.float32)
    image32 = saved["image"].astype(jnp.float32)
    output3 = saved["output"].reshape(pair_count, length, model_width)
    joined = output3.astype(jnp.bfloat16)
    text_embed32 = weights[11].astype(jnp.float32)
    image_embed32 = weights[12].astype(jnp.float32)
    text_pool = jnp.mean(text32, 1)
    image_pool = jnp.mean(image32, 1)
    text_raw = jnp.dot(text_pool, text_embed32, precision=HIGHEST)
    text_inv = lax.rsqrt(jnp.sum(text_raw * text_raw, -1, keepdims=True) + EPS)
    text_low = (text_raw * text_inv).astype(jnp.bfloat16)
    image_raw = jnp.dot(image_pool, image_embed32, precision=HIGHEST)
    image_inv = lax.rsqrt(jnp.sum(image_raw * image_raw, -1, keepdims=True) + EPS)
    image_low = (image_raw * image_inv).astype(jnp.bfloat16)
    text_piece = lax.all_gather(text_low, "dp", axis=0, tiled=True)
    image_piece = lax.all_gather(image_low, "dp", axis=0, tiled=True)
    text_scores = contract_cols(text_low, image_piece) * TEMP_INVERSE
    image_scores = contract_cols(image_low, text_piece) * TEMP_INVERSE
    text_sum = jnp.sum(jnp.exp(text_scores - TEMP_INVERSE), 1)
    image_sum = jnp.sum(jnp.exp(image_scores - TEMP_INVERSE), 1)
    text_lse = TEMP_INVERSE + jnp.log(text_sum)
    image_lse = TEMP_INVERSE + jnp.log(image_sum)
    text_low32 = text_low.astype(jnp.float32)
    image_low32 = image_low.astype(jnp.float32)
    own_ids = lax.axis_index("dp") * pair_count + jnp.arange(pair_count, dtype=jnp.int32)
    text_piece = lax.all_gather(text_low32, "dp", axis=0, tiled=True)
    image_piece = lax.all_gather(image_low32, "dp", axis=0, tiled=True)
    text_piece_lse = lax.all_gather(text_lse, "dp", axis=0, tiled=True)
    image_piece_lse = lax.all_gather(image_lse, "dp", axis=0, tiled=True)
    piece_len = text_piece.shape[0]
    match = (own_ids[:, None] == jnp.arange(piece_len, dtype=jnp.int32)[None, :]).astype(
        jnp.float32
    )
    text_scores = contract_cols(text_low, image_piece.astype(jnp.bfloat16)) * TEMP_INVERSE
    text_weights = (
        jnp.exp(text_scores - text_lse[:, None])
        + jnp.exp(text_scores - image_piece_lse[None, :])
        - 2.0 * match
    )
    image_scores = contract_cols(image_low, text_piece.astype(jnp.bfloat16)) * TEMP_INVERSE
    image_weights = (
        jnp.exp(image_scores - text_piece_lse[None, :])
        + jnp.exp(image_scores - image_lse[:, None])
        - 2.0 * match
    )
    dtext_emb = GRAD_SCALE * jnp.dot(text_weights, image_piece, precision=HIGHEST)
    dimage_emb = GRAD_SCALE * jnp.dot(image_weights, text_piece, precision=HIGHEST)
    dtext_raw = unit_back(text_raw, text_inv, dtext_emb)
    dimage_raw = unit_back(image_raw, image_inv, dimage_emb)
    grad_text_embed = jnp.dot(text_pool.T, dtext_raw, precision=HIGHEST)
    grad_image_embed = jnp.dot(image_pool.T, dimage_raw, precision=HIGHEST)
    text_extra = (jnp.dot(dtext_raw, text_embed32.T, precision=HIGHEST) / length)[:, None, :]
    image_pool_grad = jnp.dot(dimage_raw, image_embed32.T, precision=HIGHEST) / patch_count
    positions = jnp.arange(length, dtype=jnp.int32)
    slots = jnp.arange(phrase_starts.shape[1], dtype=jnp.int32)
    valid = (slots[None, :] < region_counts[:, None]).astype(jnp.float32)
    ends = phrase_starts + phrase_lengths
    inside = ((positions >= phrase_starts[..., None]) & (positions < ends[..., None])).astype(
        jnp.float32
    ) * valid[..., None]
    span_weight = inside / phrase_lengths[..., None].astype(jnp.float32)
    chosen = (
        jnp.sum(
            (box_patches[..., None] == jnp.arange(patch_count, dtype=jnp.int32)).astype(
                jnp.float32
            ),
            axis=2,
        )
        / box_patches.shape[2]
    )
    phrase = jnp.einsum("pbt,ptd->pbd", span_weight, output3, precision=HIGHEST)
    region = jnp.einsum("pbn,pnd->pbd", chosen, image32, precision=HIGHEST)
    mismatch = (phrase - region) * valid[..., None]
    box_text = jnp.einsum("pbt,pbd->ptd", span_weight, mismatch, precision=HIGHEST)
    box_image = -jnp.einsum("pbn,pbd->pnd", chosen, mismatch, precision=HIGHEST)
    image_extra = box_image + image_pool_grad[:, None, :]
    own_extra = lax.dynamic_slice_in_dim(
        image_extra, lax.axis_index("mp") * half_pairs, half_pairs, 0
    )
    weights = gather_weights(*shards)
    state = layer_forward(text, patches, weights)
    (
        query_w,
        key_w,
        value_w,
        attn_out_w,
        cross_query_w,
        cross_key_w,
        cross_value_w,
        cross_out_w,
        image_w,
        ffn_in_w,
        ffn_out_w,
        text_embed_w,
        image_embed_w,
        gain_one,
        bias_one,
        gain_two,
        bias_two,
        gain_three,
        bias_three,
    ) = weights
    upstream = cotangent.astype(jnp.float32).reshape(-1, model_width) + box_text.reshape(
        -1, model_width
    )
    grad_third, gain_three_grad, bias_three_grad = norm_back(
        upstream, state["normed_three"], state["inv_three"], gain_three.astype(jnp.float32)
    )
    low_third = grad_third.astype(jnp.bfloat16)
    grad_ffn_out = contract_rows(state["active"], low_third)
    dactive = contract_cols(low_third, ffn_out_w)
    gelu_pull = jax.vjp(lambda values: jax.nn.gelu(values, approximate=False), state["inner"])[1]
    dinner = gelu_pull(dactive)[0].astype(jnp.bfloat16)
    grad_ffn_in = contract_rows(state["low_two"], dinner)
    grad_second = grad_third + stream_sum(contract_cols(dinner, ffn_in_w))
    ffn_parts = (grad_ffn_in, grad_ffn_out, gain_three_grad, bias_three_grad)
    grad_second, gain_two_grad, bias_two_grad = norm_back(
        grad_second, state["normed_two"], state["inv_two"], gain_two.astype(jnp.float32)
    )
    low_second = grad_second.astype(jnp.bfloat16)
    grad_cross_out = contract_rows(state["cross_mixed"], low_second)
    dcross = split_heads(contract_cols(low_second, cross_out_w).astype(jnp.bfloat16), pair_count)
    dqueries, dkeys, dvalues = attend_back(
        state["cross_queries"],
        state["cross_keys"],
        state["cross_values"],
        state["cross_total"],
        dcross,
    )
    grad_cross_query = contract_rows(state["low_one"], dqueries)
    grad_first = grad_second + stream_sum(contract_cols(dqueries, cross_query_w))
    grad_cross_key = contract_rows(state["image_rows"], dkeys)
    grad_cross_value = contract_rows(state["image_rows"], dvalues)
    dimage_part = contract_cols(dkeys, cross_key_w) + contract_cols(dvalues, cross_value_w)
    dimage = (
        lax.psum_scatter(
            dimage_part.reshape(pair_count, patch_count, model_width).astype(jnp.bfloat16),
            "mp",
            scatter_dimension=0,
            tiled=True,
        ).astype(jnp.float32)
        + own_extra
    )
    low_image = dimage.astype(jnp.bfloat16).reshape(-1, model_width)
    patch_rows = patches.reshape(-1, patches.shape[2])
    grad_image_part = contract_rows(patch_rows, low_image)
    patch_grad = contract_cols(low_image, image_w).reshape(patches.shape)
    grad_first, gain_one_grad, bias_one_grad = norm_back(
        grad_first, state["normed_one"], state["inv_one"], gain_one.astype(jnp.float32)
    )
    low_first = grad_first.astype(jnp.bfloat16)
    grad_attn_out = contract_rows(state["self_mixed"], low_first)
    dself = split_heads(contract_cols(low_first, attn_out_w).astype(jnp.bfloat16), pair_count)
    dqueries, dkeys, dvalues = attend_back(
        state["queries"], state["key_heads"], state["value_heads"], state["self_total"], dself
    )
    grad_query = contract_rows(state["text_rows"], dqueries)
    grad_key = contract_rows(state["text_rows"], dkeys)
    grad_value = contract_rows(state["text_rows"], dvalues)
    dtext_part = (
        contract_cols(dqueries, query_w)
        + contract_cols(dkeys, key_w)
        + contract_cols(dvalues, value_w)
    )
    dtext_sum, grad_image = (
        lax.psum(dtext_part.astype(jnp.bfloat16), "mp").astype(jnp.float32),
        lax.psum(grad_image_part.astype(jnp.bfloat16), "mp").astype(jnp.float32),
    )
    text_grad = (grad_first + dtext_sum).reshape(pair_count, length, model_width) + text_extra
    reduced = (
        *in_one_piece(
            (
                grad_query.astype(jnp.bfloat16),
                grad_key.astype(jnp.bfloat16),
                grad_value.astype(jnp.bfloat16),
            ),
            "dp",
            0,
            1,
        ),
        sum_at_owner(grad_attn_out.astype(jnp.bfloat16), "dp", 1),
        *in_one_piece(
            (
                grad_cross_query.astype(jnp.bfloat16),
                grad_cross_key.astype(jnp.bfloat16),
                grad_cross_value.astype(jnp.bfloat16),
            ),
            "dp",
            0,
            1,
        ),
        sum_at_owner(grad_cross_out.astype(jnp.bfloat16), "dp", 1),
        sum_at_owner(grad_image.astype(jnp.bfloat16), "dp", 0),
        sum_at_owner(ffn_parts[0].astype(jnp.bfloat16), "dp", 0),
        sum_at_owner(ffn_parts[1].astype(jnp.bfloat16), "dp", 1),
        *side_by_side(
            (
                grad_text_embed.astype(jnp.bfloat16),
                grad_image_embed.astype(jnp.bfloat16),
                gain_one_grad.astype(jnp.bfloat16),
                bias_one_grad.astype(jnp.bfloat16),
                gain_two_grad.astype(jnp.bfloat16),
                bias_two_grad.astype(jnp.bfloat16),
                ffn_parts[2].astype(jnp.bfloat16),
                ffn_parts[3].astype(jnp.bfloat16),
            ),
            "dp",
            0,
            1,
        ),
    )
    return (
        joined,
        text_grad,
        patch_grad,
        reduced[0],
        reduced[1],
        reduced[2],
        reduced[3],
        reduced[4],
        reduced[5],
        reduced[6],
        reduced[7],
        reduced[8],
        reduced[9],
        reduced[10],
        reduced[11],
        reduced[12],
        reduced[13],
        reduced[14],
        reduced[15],
        reduced[16],
        reduced[17],
        reduced[18],
    )


def solution(mesh):
    in_specs = (
        P("dp", None, None),
        P(("dp", "mp"), None, None),
        P("dp", None, None),
        P("dp"),
        P("dp", None),
        P("dp", None),
        P("dp", None, None),
        P("dp", "mp"),
        P("dp", "mp"),
        P("dp", "mp"),
        P("mp", "dp"),
        P("dp", "mp"),
        P("dp", "mp"),
        P("dp", "mp"),
        P("mp", "dp"),
        P("dp", None),
        P("dp", "mp"),
        P("mp", "dp"),
        P("dp", None),
        P("dp", None),
        P("dp"),
        P("dp"),
        P("dp"),
        P("dp"),
        P("dp"),
        P("dp"),
    )
    out_specs = (
        P("dp", None, None),
        P("dp", None, None),
        P(("dp", "mp"), None, None),
        P("dp", "mp"),
        P("dp", "mp"),
        P("dp", "mp"),
        P("mp", "dp"),
        P("dp", "mp"),
        P("dp", "mp"),
        P("dp", "mp"),
        P("mp", "dp"),
        P("dp", None),
        P("dp", "mp"),
        P("mp", "dp"),
        P("dp", None),
        P("dp", None),
        P("dp"),
        P("dp"),
        P("dp"),
        P("dp"),
        P("dp"),
        P("dp"),
    )
    return jax.shard_map(body, mesh=mesh, in_specs=in_specs, out_specs=out_specs, check_vma=False)
```

profile of v0, /device:TPU:12, one launch (start us, length us, event | category | flops | bytes accessed | tf_op | source)
XLA Modules:
  0.0 1324.7 jit_solution(977948992261333085)
XLA Ops:
  8.8 35.1 %all_gather.95 = bf16[768,384]{1,0:T(8,128)(2,1)S(1)} all-gather(bf16[48,384]{1,0:T(8,128)(2,1)} %param.35), channel_id=1, replica_groups=mesh['dp'=16,'mp'=2] {'dp'}, dimensions={0}, use_global_device_ids=true | all-gather | bytes 626688 | tf_op jit(solution)/shard_map/all_gather | solution.py:162
  48.4 40.0 %all_gather.96 = bf16[768,384]{1,0:T(8,128)(2,1)S(1)} all-gather(bf16[48,384]{1,0:T(8,128)(2,1)S(1)} %copy-done.106), channel_id=1, replica_groups=mesh['dp'=16,'mp'=2] {'dp'}, dimensions={0}, use_global_device_ids=true | all-gather | bytes 626688 | tf_op jit(solution)/shard_map/all_gather | solution.py:160
  91.8 41.3 %all_gather.97 = bf16[768,384]{1,0:T(8,128)(2,1)S(1)} all-gather(bf16[48,384]{1,0:T(8,128)(2,1)S(1)} %copy-done.107), channel_id=1, replica_groups=mesh['dp'=16,'mp'=2] {'dp'}, dimensions={0}, use_global_device_ids=true | all-gather | bytes 626688 | tf_op jit(solution)/shard_map/all_gather | solution.py:161
  146.0 38.9 %all_gather.98 = bf16[384,768]{0,1:T(8,128)(2,1)S(1)} all-gather(bf16[384,48]{0,1:T(8,128)(2,1)S(1)} %copy-done.108), channel_id=1, replica_groups=mesh['dp'=16,'mp'=2] {'dp'}, dimensions={1}, use_global_device_ids=true | all-gather | bytes 626688 | tf_op jit(solution)/shard_map/all_gather | solution.py:163
  190.7 73.6 %all-reduce.9 = (bf16[768]{0:T(1024)(128)(2,1)S(1)}, bf16[768]{0:T(1024)(128)(2,1)S(1)}, bf16[768]{0:T(1024)(128)(2,1)S(1)}, bf16[768]{0:T(1024)(128)(2,1)S(1)},...) all-reduce(bf16[768]{0:T(1024)(128)(2,1)S(1)} %dynamic-update-slice., ...), channel_id=1, replica_groups=mesh['dp'=16,'mp'=2] {'dp'}, use_global_device_ids=true, to_apply=%add.1 | all-reduce | flops 4608 | bytes 18432
  270.9 41.4 %all_gather.104 = bf16[768,384]{1,0:T(8,128)(2,1)} all-gather(bf16[48,384]{1,0:T(8,128)(2,1)S(1)} %copy-done.109), channel_id=1, replica_groups=mesh['dp'=16,'mp'=2] {'dp'}, dimensions={0}, use_global_device_ids=true | all-gather | bytes 626688 | tf_op jit(solution)/shard_map/all_gather | solution.py:164
  312.3 43.2 %all_gather.105 = bf16[768,384]{1,0:T(8,128)(2,1)} all-gather(bf16[48,384]{1,0:T(8,128)(2,1)S(1)} %copy-done.110), channel_id=1, replica_groups=mesh['dp'=16,'mp'=2] {'dp'}, dimensions={0}, use_global_device_ids=true | all-gather | bytes 626688 | tf_op jit(solution)/shard_map/all_gather | solution.py:165
  355.5 41.6 %all_gather.103 = bf16[768,384]{1,0:T(8,128)(2,1)} all-gather(bf16[48,384]{1,0:T(8,128)(2,1)S(1)} %copy-done.111), channel_id=1, replica_groups=mesh['dp'=16,'mp'=2] {'dp'}, dimensions={0}, use_global_device_ids=true | all-gather | bytes 626688 | tf_op jit(solution)/shard_map/all_gather | solution.py:166
  397.0 40.6 %all_gather.106 = bf16[384,768]{0,1:T(8,128)(2,1)S(1)} all-gather(bf16[384,48]{0,1:T(8,128)(2,1)S(1)} %copy-done.112), channel_id=1, replica_groups=mesh['dp'=16,'mp'=2] {'dp'}, dimensions={1}, use_global_device_ids=true | all-gather | bytes 626688 | tf_op jit(solution)/shard_map/all_gather | solution.py:167
  501.4 24.5 %all-reduce.20.cloned.1.call-done = f32[732,768]{1,0:T(8,128)} async-done(((f32[732,768]{1,0:T(8,128)}), f32[732,768]{1,0:T(8,128)}) %all-reduce.20.cloned.1.call-update) | async-done | bytes 2248720 | tf_op jit(solution)/shard_map/psum | solution.py:131
  531.6 39.1 %all-gather.13.cloned.1.call-done = bf16[768,1536]{1,0:T(8,128)(2,1)} async-done(((bf16[48,1536]{1,0:T(8,128)(2,1)}), bf16[768,1536]{1,0:T(8,128)(2,1)}) %all-gather.13.cloned.1.call-update) | async-done | bytes 2359312 | tf_op jit(solution)/shard_map/all_gather | solution.py:169
  570.7 15.2 %multiply_convert_fusion.2 = (bf16[732,1536]{1,0:T(8,128)(2,1)}, f32[732,1536]{1,0:T(8,128)}, f32[732,1536]{1,0:T(8,128)}) fusion(bf16[768,1536]{1,0:T(8,128)(2,1)} %all-gather.13.cloned.1.call-done, f32[732,768]{1,0:T(8,128)} %get-tuple-element.59, f32[768]{0:T(1024)S(1)} %convert_element_type.414, f32[768]{0:T(1024)S(1)} %convert_element_type.413, ...), kind=kOutput, calls=%fused_computation.13 | convolution fusion | flops 1802898432 | bytes 15863520 | tf_op jit(solution)/shard_map/dot_general | solution.py:48
  586.0 48.7 %all-gather.15.cloned.1.call-done = bf16[1536,768]{0,1:T(8,128)(2,1)} async-done(((bf16[1536,48]{0,1:T(8,128)(2,1)}), bf16[1536,768]{0,1:T(8,128)(2,1)}) %all-gather.15.cloned.1.call-update) | async-done | bytes 2359312 | tf_op jit(solution)/shard_map/all_gather | solution.py:170
  642.7 30.8 %all_gather.113 = bf16[768,256]{1,0:T(8,128)(2,1)S(1)} all-gather(bf16[48,256]{1,0:T(8,128)(2,1)S(1)} %copy-done.113), channel_id=1, replica_groups=mesh['dp'=16,'mp'=2] {'dp'}, dimensions={0}, use_global_device_ids=true | all-gather | bytes 417792 | tf_op jit(solution)/shard_map/all_gather | solution.py:171
  675.3 36.0 %all-gather.2 = bf16[16,12,256]{2,1,0:T(8,128)(2,1)S(1)} all-gather(bf16[1,12,256]{2,1,0:T(8,128)(2,1)S(1)} %bitcast.160), channel_id=1, replica_groups=mesh['dp'=16,'mp'=2] {'dp'}, dimensions={0}, use_global_device_ids=true | all-gather | bytes 104448 | tf_op jit(solution)/shard_map/all_gather | solution.py:332
  712.0 39.3 %all-gather.3 = f32[16,12,256]{2,1,0:T(8,128)S(1)} all-gather(f32[1,12,256]{2,1,0:T(8,128)S(1)} %get-tuple-element.52), channel_id=1, replica_groups=mesh['dp'=16,'mp'=2] {'dp'}, dimensions={0}, use_global_device_ids=true | all-gather | bytes 208896 | tf_op jit(solution)/shard_map/all_gather | solution.py:343
  752.9 38.1 %all_gather.114 = bf16[768,256]{1,0:T(8,128)(2,1)S(1)} all-gather(bf16[48,256]{1,0:T(8,128)(2,1)S(1)} %copy-done.114), channel_id=1, replica_groups=mesh['dp'=16,'mp'=2] {'dp'}, dimensions={0}, use_global_device_ids=true | all-gather | bytes 417792 | tf_op jit(solution)/shard_map/all_gather | solution.py:172
  834.6 41.2 %all-gather = f32[16,12,256]{2,1,0:T(8,128)} all-gather(f32[1,12,256]{2,1,0:T(8,128)S(1)} %get-tuple-element.50), channel_id=1, replica_groups=mesh['dp'=16,'mp'=2] {'dp'}, dimensions={0}, use_global_device_ids=true | all-gather | bytes 208896 | tf_op jit(solution)/shard_map/all_gather | solution.py:344
  914.3 38.5 %all-gather.1 = bf16[16,12,256]{2,1,0:T(8,128)(2,1)} all-gather(bf16[1,12,256]{2,1,0:T(8,128)(2,1)S(1)} %bitcast.161), channel_id=1, replica_groups=mesh['dp'=16,'mp'=2] {'dp'}, dimensions={0}, use_global_device_ids=true | all-gather | bytes 104448 | tf_op jit(solution)/shard_map/all_gather | solution.py:333
  957.4 39.9 %all-reduce.8 = (f32[192]{0:T(256)}, f32[192]{0:T(256)}) all-reduce(f32[192]{0:T(256)S(1)} %get-tuple-element.80, f32[192]{0:T(256)S(1)} %get-tuple-element.76), channel_id=1, replica_groups=mesh['dp'=16,'mp'=2] {'dp'}, use_global_device_ids=true, to_apply=%add.6 | all-reduce | flops 384 | bytes 3072
  1003.4 13.7 %all-to-all-start.3 = ((bf16[16,384,48]{1,2,0:T(8,128)(2,1)}), bf16[16,384,48]{1,2,0:T(8,128)(2,1)S(1)}, u32[]{:S(2)}, u32[]{:S(2)}) async-start(bf16[16,384,48]{1,2,0:T(8,128)(2,1)} %bitcast.157), calls=%async_computation.4 | async-start | bytes 1179648 | tf_op jit(solution)/shard_map/all_to_all | solution.py:25
  1068.5 25.0 %all-to-all-done.7 = bf16[16,48,518]{2,1,0:T(8,128)(2,1)S(1)} async-done(((bf16[16,48,518]{2,1,0:T(8,128)(2,1)}), bf16[16,48,518]{2,1,0:T(8,128)(2,1)S(1)}, u32[]{:S(2)}, u32[]{:S(2)}) %all-to-all-start.7) | async-done | bytes 795680 | tf_op jit(solution)/shard_map/all_to_all | solution.py:25
  1105.5 24.7 %all-to-all-done.5 = bf16[16,48,1536]{2,1,0:T(8,128)(2,1)} async-done(((bf16[16,48,1536]{2,1,0:T(8,128)(2,1)}), bf16[16,48,1536]{2,1,0:T(8,128)(2,1)}, u32[]{:S(2)}, u32[]{:S(2)}) %all-to-all-start.5) | async-done | bytes 2359328 | tf_op jit(solution)/shard_map/all_to_all | solution.py:25
  1298.6 16.2 %all-to-all-done.4 = bf16[16,64,768]{2,1,0:T(8,128)(2,1)} async-done(((bf16[16,64,768]{2,1,0:T(8,128)(2,1)}), bf16[16,64,768]{2,1,0:T(8,128)(2,1)}, u32[]{:S(2)}, u32[]{:S(2)}) %all-to-all-start.4) | async-done | bytes 1572896 | tf_op jit(solution)/shard_map/all_to_all | solution.py:25
  (549 shorter events, 439.3 us)
Async XLA Ops:
  8.0 258.3 %all-gather.9.cloned.1.call-start = ((), (), s32[]{:S(2)}) async-start(), calls=%async_computation.10 | async-start | bytes 1671168 | tf_op jit(solution)/shard_map/all_gather | solution.py:168
  8.8 428.9 %all-reduce.18.cloned.1.call-start = ((), (), s32[]{:S(2)}) async-start(), calls=%async_computation.9 | async-start | bytes 4521984 | tf_op jit(solution)/shard_map/psum | solution.py:131
  187.9 260.8 %all-gather.11.cloned.1.call-start = ((), (), s32[]{:S(2)}) async-start(), calls=%async_computation.11 | async-start | bytes 4202496 | tf_op jit(solution)/shard_map/all_gather | solution.py:211
  264.2 261.6 %copy-start.90 = (f32[768]{0:T(1024)}, f32[768]{0:T(1024)S(1)}, u32[]{:S(2)}) copy-start(f32[768]{0:T(1024)S(1)} %convert_element_type.403) | copy-start | bytes 9220
  270.8 255.0 %all-reduce.20.cloned.1.call-start = ((), (), s32[]{:S(2)}) async-start(), calls=%async_computation.12 | async-start | bytes 4521984 | tf_op jit(solution)/shard_map/psum | solution.py:131
  498.8 71.9 %all-gather.13.cloned.1.call-start = ((), (), s32[]{:S(2)}) async-start(), calls=%async_computation.13 | async-start | bytes 2506752 | tf_op jit(solution)/shard_map/all_gather | solution.py:169
  499.6 135.1 %all-gather.15.cloned.1.call-start = ((), (), s32[]{:S(2)}) async-start(), calls=%async_computation.14 | async-start | bytes 2506752 | tf_op jit(solution)/shard_map/all_gather | solution.py:170
  500.3 295.1 %all-reduce.22.cloned.1.call-start = ((), (), s32[]{:S(2)}) async-start(), calls=%async_computation.15 | async-start | bytes 4521984 | tf_op jit(solution)/shard_map/psum | solution.py:131
  501.3 381.6 %copy-start.97 = (f32[768]{0:T(1024)}, f32[768]{0:T(1024)S(1)}, u32[]{:S(2)}) copy-start(f32[768]{0:T(1024)S(1)} %convert_element_type.413) | copy-start | bytes 9220
  501.3 294.1 %copy-start.116 = (f32[768]{0:T(1024)}, f32[768]{0:T(1024)S(1)}, u32[]{:S(2)}) copy-start(f32[768]{0:T(1024)S(1)} %convert_element_type.414) | copy-start | bytes 9220
  529.5 353.3 %copy-start.94 = (f32[732]{0:T(1024)}, f32[732]{0:T(1024)S(1)}, u32[]{:S(2)}) copy-start(f32[732]{0:T(1024)S(1)} %broadcast_multiply_fusion.7) | copy-start | bytes 8788
  531.6 263.8 %copy-start.99 = (f32[732]{0:T(1024)}, f32[732]{0:T(1024)S(1)}, u32[]{:S(2)}) copy-start(f32[732]{0:T(1024)S(1)} %add_rsqrt_fusion.1) | copy-start | bytes 8788
  640.4 238.0 %all-reduce.24.cloned.1.call-start = ((), (), s32[]{:S(2)}) async-start(), calls=%async_computation.16 | async-start | bytes 2260992 | tf_op jit(solution)/shard_map/psum | solution.py:135
  831.3 185.8 %all-reduce.26.cloned.1.call-start = ((), (), s32[]{:S(2)}) async-start(), calls=%async_computation.17 | async-start | bytes 2260992 | tf_op jit(solution)/shard_map/psum | solution.py:135
  1003.4 24.0 %all-to-all-start.3 = ((bf16[16,384,48]{1,2,0:T(8,128)(2,1)}), bf16[16,384,48]{1,2,0:T(8,128)(2,1)S(1)}, u32[]{:S(2)}, u32[]{:S(2)}) async-start(bf16[16,384,48]{1,2,0:T(8,128)(2,1)} %bitcast.157), calls=%async_computation.4 | async-start | bytes 1179648 | tf_op jit(solution)/shard_map/all_to_all | solution.py:25
  1027.4 26.5 %all-to-all-start.1 = ((bf16[16,384,48]{1,2,0:T(8,128)(2,1)}), bf16[16,384,48]{1,2,0:T(8,128)(2,1)S(1)}, u32[]{:S(2)}, u32[]{:S(2)}) async-start(bf16[16,384,48]{1,2,0:T(8,128)(2,1)} %bitcast.20), calls=%async_computation.2 | async-start | bytes 1179648 | tf_op jit(solution)/shard_map/all_to_all | solution.py:25
  1054.7 38.8 %all-to-all-start.7 = ((bf16[16,48,518]{2,1,0:T(8,128)(2,1)}), bf16[16,48,518]{2,1,0:T(8,128)(2,1)S(1)}, u32[]{:S(2)}, u32[]{:S(2)}) async-start(bf16[16,48,518]{2,1,0:T(8,128)(2,1)} %concatenate.18), calls=%async_computation.8 | async-start | bytes 1966080 | tf_op jit(solution)/shard_map/all_to_all | solution.py:25
  1094.4 35.8 %all-to-all-start.5 = ((bf16[16,48,1536]{2,1,0:T(8,128)(2,1)}), bf16[16,48,1536]{2,1,0:T(8,128)(2,1)}, u32[]{:S(2)}, u32[]{:S(2)}) async-start(bf16[16,48,1536]{2,1,0:T(8,128)(2,1)} %bitcast.156), calls=%async_computation.6 | async-start | bytes 4718592 | tf_op jit(solution)/shard_map/all_to_all | solution.py:25
  1130.2 60.1 %all-to-all-start.6 = ((bf16[16,1536,48]{1,2,0:T(8,128)(2,1)}), bf16[16,1536,48]{1,2,0:T(8,128)(2,1)}, u32[]{:S(2)}, u32[]{:S(2)}) async-start(bf16[16,1536,48]{1,2,0:T(8,128)(2,1)} %bitcast.155), calls=%async_computation.7 | async-start | bytes 4718592 | tf_op jit(solution)/shard_map/all_to_all | solution.py:25
  1135.4 104.1 %reduce-scatter.2.cloned.1.call-start = ((), (), s32[]{:S(2)}) async-start(), calls=%async_computation.18 | async-start | bytes 4202496 | tf_op jit(solution)/shard_map/reduce_scatter | solution.py:453
  1190.3 41.9 %all-to-all-start.2 = ((bf16[16,48,1152]{2,1,0:T(8,128)(2,1)}), bf16[16,48,1152]{2,1,0:T(8,128)(2,1)}, u32[]{:S(2)}, u32[]{:S(2)}) async-start(bf16[16,48,1152]{2,1,0:T(8,128)(2,1)} %bitcast.153), calls=%async_computation.3 | async-start | bytes 3538944 | tf_op jit(solution)/shard_map/all_to_all | solution.py:25
  1232.2 31.1 %all-to-all-start = ((bf16[16,48,1152]{2,1,0:T(8,128)(2,1)}), bf16[16,48,1152]{2,1,0:T(8,128)(2,1)}, u32[]{:S(2)}, u32[]{:S(2)}) async-start(bf16[16,48,1152]{2,1,0:T(8,128)(2,1)} %bitcast.18), calls=%async_computation.1 | async-start | bytes 3538944 | tf_op jit(solution)/shard_map/all_to_all | solution.py:25
  1239.2 31.1 %all-reduce.28.cloned.1.call-start = ((), (), s32[]{:S(2)}) async-start(), calls=%async_computation.19 | async-start | bytes 5406720 | tf_op jit(solution)/shard_map/psum | solution.py:483
  1270.3 44.5 %all-to-all-start.4 = ((bf16[16,64,768]{2,1,0:T(8,128)(2,1)}), bf16[16,64,768]{2,1,0:T(8,128)(2,1)}, u32[]{:S(2)}, u32[]{:S(2)}) async-start(bf16[16,64,768]{2,1,0:T(8,128)(2,1)} %get-tuple-element.49), calls=%async_computation.5 | async-start | bytes 3145728 | tf_op jit(solution)/shard_map/all_to_all | solution.py:25
  (147 other events, 2279.5 us)
Sparse Core Ops, SparseCore 0:
  11.6 59.5 all-gather.8
  502.5 68.1 all-gather.12
  573.5 61.0 all-gather.14
Sparse Core Ops, SparseCore 1:
  188.0 28.7 all-reduce.17
  270.9 17.5 all-gather.10
  498.9 26.9 all-reduce.19
  640.4 19.8 all-reduce.21
  831.4 27.2 all-reduce.23
  914.4 25.4 all-reduce.25
  1169.7 11.5 reduce-scatter.1
  1247.1 23.2 all-reduce.27
where the time goes:
time: 1340 us; the launch traced here: 1320 us
  blocking collectives  659 us (49%)
  waiting for transfers between devices  215 us (16%)
  matrix products  152 us (11%)
  local copies, waits for them, and re-layouts  151 us (11%)
  other arithmetic  69 us (5%)
  starting transfers between devices  60.1 us (4%)
  between operations  18.9 us (1%)
    unnamed x2, blocking collectives  113 us
    all_to_all x8, waiting for transfers between devices, sum_at_owner(): lax.all_to_all(parts, axis, split_axis=0, concat_axis=0, tiled=True)  93.1 us
    all_to_all x8, starting transfers between devices, sum_at_owner(): lax.all_to_all(parts, axis, split_axis=0, concat_axis=0, tiled=True)  59.2 us
    all_gather x1, waiting for transfers between devices, gather_weights(): lax.all_gather(ffn_out_w, 'dp', axis=1, tiled=True)  48.7 us
    all_gather x1, blocking collectives, gather_weights(): lax.all_gather(cross_key_w, 'dp', axis=0, tiled=True)  43.2 us
    reshape x15, local copies, waits for them, and re-layouts, split_heads(): return flat.reshape(pair_count, -1, flat.shape[-1] // HEAD_DIM, HEAD_DIM)  42.8 us
    dot_general x11, matrix products, matmul(): return jnp.dot(left, right, preferred_element_type=jnp.float32)  41.6 us
    all_gather x1, blocking collectives, gather_weights(): lax.all_gather(cross_value_w, 'dp', axis=0, tiled=True)  41.6 us
  transfers between devices with their start and end apart: 19, of which 10 were waited for; matrix products, arithmetic and copies ran while one was open for 17% of the time, Pallas kernels for 0%

commit v1 on v0

v1 whole, which is shorter than its diff:
```python
import functools
import math

import jax
import jax.numpy as jnp
from jax import lax
from jax.experimental import pallas as pl
from jax.experimental.pallas import tpu as pltpu
from jax.sharding import PartitionSpec as P

HEAD_DIM = 64
EPS = 1e-06
TEMP_INVERSE = 20.0
GRAD_SCALE = 10.0
HIGHEST = lax.Precision.HIGHEST
MESH = pl.DeviceIdType.MESH
BF16 = jnp.bfloat16
F32 = jnp.float32


def split_dims(count):
    side = math.isqrt(count // 4) if count % 4 == 0 else 0
    if side and 4 * side * side == count:
        return (4, side, side)
    return (count, 1, 1)


class Place:
    def __init__(self, dims):
        self.dims = dims
        dp = lax.axis_index("dp")
        self.mp = lax.axis_index("mp")
        self.pos = (dp // (dims[1] * dims[2]), (dp // dims[2]) % dims[1], dp % dims[2])

    def at(self, axis, coord):
        spot = list(self.pos)
        spot[axis] = coord
        return ((spot[0] * self.dims[1] + spot[1]) * self.dims[2] + spot[2], self.mp)

    def peer(self):
        return (lax.axis_index("dp"), 1 - self.mp)


def block_of(place, order, stage, coord):
    index = [None] * 3
    for rank, axis in enumerate(order):
        index[axis] = slice(None) if rank < stage else (coord if rank == stage else place.pos[axis])
    return tuple(index)


def remote(src, dst, send_sem, recv_sem, device):
    return pltpu.make_async_remote_copy(
        src_ref=src,
        dst_ref=dst,
        send_sem=send_sem,
        recv_sem=recv_sem,
        device_id=device,
        device_id_type=MESH,
    )


def greet_lines(place):
    sem = pltpu.get_barrier_semaphore()

    def greet(device):
        pl.semaphore_signal(sem, inc=1, device_id=device, device_id_type=MESH)

    greet(place.peer())
    count = 1
    for axis in range(3):
        for away in range(1, place.dims[axis]):
            greet(place.at(axis, lax.rem(place.pos[axis] + away, place.dims[axis])))
            count += 1
    pl.semaphore_wait(sem, count)


def gather_steps(place, order, buf, send_sem, recv_sem):
    sent = []
    for stage, axis in enumerate(order):
        length, pos = place.dims[axis], place.pos[axis]
        if length == 1:
            continue

        def copy(way, step, coord, stage=stage, axis=axis, pos=pos):
            ref = buf.at[block_of(place, order, stage, coord)]
            device = place.at(axis, pos + 1 if way == 0 else pos - 1)
            return remote(ref, ref, send_sem.at[axis, way, step - 1], recv_sem.at[axis, way, step - 1], device)

        for step in range(1, length + 1):
            for way in (0, 1):
                coord = pos - (step - 1) if way == 0 else pos + (step - 1)
                here = (coord >= 0) if way == 0 else (coord < length)
                if step > 1:
                    pl.when(here)(lambda: copy(way, step - 1, coord).wait_recv())
                if step < length:
                    more = jnp.logical_and(here, (pos + 1 < length) if way == 0 else (pos > 0))
                    pl.when(more)(lambda: copy(way, step, coord).start())
                    sent.append((more, functools.partial(copy, way, step, coord)))
            if step < length:
                yield
    return sent


def scatter_steps(place, order, acc, arrive, send_sem, recv_sem, result):
    sent = []
    last = [axis for axis in order if place.dims[axis] > 1][0]
    at = 0
    for stage in reversed(range(3)):
        axis = order[stage]
        length, pos = place.dims[axis], place.pos[axis]
        if length == 1:
            continue
        units = math.prod(place.dims[a] for a in order[:stage])
        shape = tuple(place.dims[a] for a in sorted(order[:stage]))

        def copy(way, step, coord, stage=stage, axis=axis, pos=pos, at=at, units=units, length=length, shape=shape):
            src = acc.at[block_of(place, order, stage, coord)]
            slot = at + (way * (length - 1) + step - 1) * units
            dst = arrive.at[pl.ds(slot, units)].reshape(*shape, *arrive.shape[1:])
            device = place.at(axis, pos + 1 if way == 0 else pos - 1)
            return (
                remote(src, dst, send_sem.at[axis, way, step - 1], recv_sem.at[axis, way, step - 1], device),
                dst,
            )

        for step in range(length - 1, 0, -1):
            for way in (0, 1):
                coord = pos + step if way == 0 else pos - step
                has = (coord < length) if way == 0 else (coord >= 0)
                pl.when(has)(lambda: copy(way, step, coord)[0].start())
                sent.append((has, functools.partial(lambda move, *a: move(*a)[0], copy, way, step, coord)))
            yield
            for way in (0, 1):
                coord = pos - 1 + step if way == 0 else pos + 1 - step
                comes = jnp.logical_and(pos > 0, coord < length) if way == 0 else jnp.logical_and(pos < length - 1, coord >= 0)

                def take():
                    move, ref = copy(way, step, coord)
                    move.wait_recv()
                    index = block_of(place, order, stage, coord)
                    total = acc[index].astype(F32) + ref[...].astype(F32)
                    if axis == last and step == 1:
                        result[...] = total
                    acc[index] = total.astype(BF16)

                pl.when(comes)(take)
        at += 2 * (length - 1) * units
    return sent


def arrive_units(dims, order):
    units = 0
    for stage in range(3):
        if dims[order[stage]] > 1:
            units += 2 * (dims[order[stage]] - 1) * math.prod(dims[a] for a in order[:stage])
    return units


def in_turn(plan):
    events = sorted((time, which, step) for which, (times, _) in enumerate(plan) for step, time in enumerate(times))
    results = [None] * len(plan)
    for _, which, _ in events:
        if results[which] is None:
            try:
                next(plan[which][1])
            except StopIteration as stop:
                results[which] = stop.value
    assert all(r is not None for r in results)
    return results


def wait_sent(sent):
    for cond, make in sent:
        if cond is None:
            make().wait_send()
        else:
            pl.when(cond)(lambda: make().wait_send())


ORDERS = ((2, 0, 1), (1, 0, 2), (0, 2, 1), (2, 0, 1), (1, 0, 2), (0, 1, 2))


def step_times(dims, order, start, back=False):
    times = [0.0]
    units = 1
    for axis in order:
        for _ in range(dims[axis] - 1):
            times.append(times[-1] + 1.6 * units + 3.0)
        units *= dims[axis]
    times.append(times[-1] + 4.0)
    if back:
        times = [times[-1] - t for t in reversed(times)]
    return [start + t for t in times] + [start + times[-1] + 4.0, start + times[-1] + 8.0]


def gather_kernel(dims, count, *refs):
    ins, outs = refs[:count], refs[count : 2 * count]
    send_sem, recv_sem, own_sem, peer_send, peer_recv = refs[2 * count :]
    place = Place(dims)
    own = [
        pltpu.make_async_copy(ins[c], outs[c].at[(place.mp,) + place.pos], own_sem.at[c]) for c in range(count)
    ]
    for copy in own:
        copy.start()
    greet_lines(place)

    def chunk(c, order):
        own[c].wait()
        mine, other = outs[c].at[place.mp], outs[c].at[1 - place.mp]
        sent = yield from gather_steps(place, order, mine, send_sem.at[c], recv_sem.at[c])

        def copy(ref):
            return remote(ref, ref, peer_send.at[c], peer_recv.at[c], place.peer())

        copy(mine).start()
        yield
        copy(other).wait_recv()
        return sent + [(None, lambda: copy(mine))]

    plan = []
    for c in range(count):
        order = ORDERS[c % len(ORDERS)]
        plan.append((step_times(dims, order, 3.9 * c), chunk(c, order)))
    for sent in in_turn(plan):
        wait_sent(sent)


def gather(shards, dims):
    count = len(shards)
    longest = max(max(dims) - 1, 1)
    return pl.pallas_call(
        functools.partial(gather_kernel, dims, count),
        out_shape=[jax.ShapeDtypeStruct((2,) + dims + s.shape, BF16) for s in shards],
        in_specs=[pl.BlockSpec(memory_space=pl.ANY)] * count,
        out_specs=[pl.BlockSpec(memory_space=pl.ANY)] * count,
        scratch_shapes=[pltpu.SemaphoreType.DMA((count, 3, 2, longest))] * 2 + [pltpu.SemaphoreType.DMA((count,))] * 3,
        compiler_params=pltpu.CompilerParams(collective_id=0, has_side_effects=True),
        name="gather_weights",
    )(*shards)


def scatter_kernel(dims, count, shared, extra, *refs):
    ins, pieces = refs[:count], refs[count : count + extra]
    refs = refs[count + extra :]
    outs, wholes = refs[:count], refs[count : count + extra]
    refs = refs[count + extra :]
    acc, peer_in, arrive = refs[:count], refs[count : 2 * count], refs[2 * count : 3 * count]
    send_sem, recv_sem, own_sem, peer_send, peer_recv, end_send, end_recv, ex_own, ex_send, ex_recv = refs[3 * count :]
    place = Place(dims)
    own = [pltpu.make_async_copy(ins[c].at[place.mp], acc[c], own_sem.at[c]) for c in range(count)]
    for copy in own:
        copy.start()
    keep = [pltpu.make_async_copy(pieces[e], wholes[e].at[place.mp], ex_own.at[e]) for e in range(extra)]
    for copy in keep:
        copy.start()
    greet_lines(place)
    give = [
        remote(pieces[e], wholes[e].at[place.mp], ex_send.at[e], ex_recv.at[e], place.peer()) for e in range(extra)
    ]

    def chunk(c, order):
        def copy():
            return remote(ins[c].at[1 - place.mp], peer_in[c], peer_send.at[c], peer_recv.at[c], place.peer())

        copy().start()
        yield
        own[c].wait()
        copy().wait_recv()
        acc[c][...] = (acc[c][...].astype(F32) + peer_in[c][...].astype(F32)).astype(BF16)
        result = outs[c].at[place.mp] if c in shared else outs[c]
        sent = yield from scatter_steps(
            place, order, acc[c], arrive[c], send_sem.at[c], recv_sem.at[c], result
        )
        sent.append((None, copy))
        if c in shared:

            def hand(half):
                ref = outs[c].at[half]
                return remote(ref, ref, end_send.at[c], end_recv.at[c], place.peer())

            hand(place.mp).start()
            yield
            hand(1 - place.mp).wait_recv()
            sent.append((None, lambda: hand(place.mp)))
        return sent

    plan = []
    for c in range(count):
        order = ORDERS[c % len(ORDERS)]
        plan.append((step_times(dims, order, 3.9 * c, True), chunk(c, order)))
    for copy in give:
        copy.start()
    for sent in in_turn(plan):
        wait_sent(sent)
    for copy in keep:
        copy.wait()
    for copy in give:
        copy.wait()


def scatter(grads, shared, pieces, dims):
    count, extra = len(grads), len(pieces)
    longest = max(max(dims) - 1, 1)
    shapes = [
        jax.ShapeDtypeStruct(((2,) if c in shared else ()) + g.shape[-2:], F32) for c, g in enumerate(grads)
    ]
    wholes = [jax.ShapeDtypeStruct((2,) + p.shape, p.dtype) for p in pieces]
    return pl.pallas_call(
        functools.partial(scatter_kernel, dims, count, shared, extra),
        out_shape=shapes + wholes,
        in_specs=[pl.BlockSpec(memory_space=pl.ANY)] * (count + extra),
        out_specs=[pl.BlockSpec(memory_space=pltpu.VMEM)] * count + [pl.BlockSpec(memory_space=pl.ANY)] * extra,
        scratch_shapes=[pltpu.VMEM(g.shape[1:], BF16) for g in grads] * 2
        + [
            pltpu.VMEM((arrive_units(dims, ORDERS[c % len(ORDERS)]),) + g.shape[-2:], BF16)
            for c, g in enumerate(grads)
        ]
        + [pltpu.SemaphoreType.DMA((count, 3, 2, longest))] * 2
        + [pltpu.SemaphoreType.DMA((count,))] * 5
        + [pltpu.SemaphoreType.DMA((extra,))] * 3,
        compiler_params=pltpu.CompilerParams(
            collective_id=1, has_side_effects=True, vmem_limit_bytes=60 * 2**20
        ),
        name="scatter_gradients",
    )(*grads, *pieces)


def matmul(left, right):
    return jnp.dot(left, right, preferred_element_type=F32)


def contract_rows(left, right):
    return lax.dot_general(left, right, (((0,), (0,)), ((), ())), preferred_element_type=F32)


def contract_cols(left, right):
    return lax.dot_general(left, right, (((1,), (1,)), ((), ())), preferred_element_type=F32)


def layer_norm(inputs, gain, shift):
    centred = inputs - jnp.mean(inputs, -1, keepdims=True)
    inv_std = lax.rsqrt(jnp.mean(centred * centred, -1, keepdims=True) + EPS)
    normed = centred * inv_std
    return (normed * gain + shift, normed, inv_std)


def norm_back(upstream, normed, inv_std, gain):
    scaled = upstream * gain
    inner_mean = jnp.mean(scaled * normed, -1, keepdims=True)
    result = inv_std * (scaled - jnp.mean(scaled, -1, keepdims=True) - normed * inner_mean)
    return (result, jnp.sum(upstream * normed, 0), jnp.sum(upstream, 0))


def split_heads(flat, pair_count):
    return flat.reshape(pair_count, -1, flat.shape[-1] // HEAD_DIM, HEAD_DIM)


def attend(queries, key_heads, value_heads):
    factor = 1.0 / math.sqrt(HEAD_DIM)
    scores = jnp.einsum("pqhd,pkhd->phqk", queries, key_heads, preferred_element_type=F32) * factor
    row_max = jnp.max(scores, -1, keepdims=True)
    expd = jnp.exp(scores - row_max)
    row_sum = jnp.sum(expd, -1, keepdims=True)
    probs = (expd / row_sum).astype(BF16)
    mixed = jnp.einsum("phqk,pkhd->pqhd", probs, value_heads, preferred_element_type=F32)
    flat_rows = queries.shape[0] * queries.shape[1]
    return (mixed.astype(BF16).reshape(flat_rows, -1), row_max + jnp.log(row_sum))


def attend_back(queries, key_heads, value_heads, log_total, upstream):
    factor = 1.0 / math.sqrt(HEAD_DIM)
    scores = jnp.einsum("pqhd,pkhd->phqk", queries, key_heads, preferred_element_type=F32) * factor
    probs = jnp.exp(scores - log_total)
    dprobs = jnp.einsum("pqhd,pkhd->phqk", upstream, value_heads, preferred_element_type=F32)
    dscores = (probs * (dprobs - jnp.sum(dprobs * probs, -1, keepdims=True))).astype(BF16)
    dqueries = jnp.einsum("phqk,pkhd->pqhd", dscores, key_heads, preferred_element_type=F32) * factor
    dkeys = jnp.einsum("phqk,pqhd->pkhd", dscores, queries, preferred_element_type=F32) * factor
    dvalues = jnp.einsum("phqk,pqhd->pkhd", probs.astype(BF16), upstream, preferred_element_type=F32)
    return tuple(t.astype(BF16).reshape(-1, t.shape[2] * t.shape[3]) for t in (dqueries, dkeys, dvalues))


def unit_back(raw, inv_norm, upstream):
    cubed = inv_norm * inv_norm * inv_norm
    return inv_norm * upstream - raw * cubed * jnp.sum(raw * upstream, -1, keepdims=True)


def contrast(text_pool, image_pool, text_embed32, image_embed32):
    text_raw = jnp.dot(text_pool, text_embed32, precision=HIGHEST)
    text_inv = lax.rsqrt(jnp.sum(text_raw * text_raw, -1, keepdims=True) + EPS)
    image_raw = jnp.dot(image_pool, image_embed32, precision=HIGHEST)
    image_inv = lax.rsqrt(jnp.sum(image_raw * image_raw, -1, keepdims=True) + EPS)
    both = jnp.concatenate([(text_raw * text_inv).astype(BF16), (image_raw * image_inv).astype(BF16)], 1)
    width = text_raw.shape[1]
    everyone = lax.all_gather(both, ("dp", "mp"), axis=0, tiled=True)
    text_all, image_all = everyone[:, :width], everyone[:, width:]
    logits = contract_cols(text_all, image_all) * TEMP_INVERSE
    weights = jnp.exp(logits - jax.nn.logsumexp(logits, axis=1, keepdims=True)) + jnp.exp(
        logits - jax.nn.logsumexp(logits, axis=0, keepdims=True)
    )
    weights = weights - 2.0 * jnp.eye(logits.shape[0], dtype=F32)
    count = text_pool.shape[0]
    start = (lax.axis_index("dp") * 2 + lax.axis_index("mp")) * count
    rows = lax.dynamic_slice_in_dim(weights, start, count, 0)
    columns = lax.dynamic_slice_in_dim(weights, start, count, 1)
    dtext = GRAD_SCALE * jnp.dot(rows, image_all.astype(F32), precision=HIGHEST)
    dimage = GRAD_SCALE * jnp.dot(columns.T, text_all.astype(F32), precision=HIGHEST)
    dtext_raw = unit_back(text_raw, text_inv, dtext)
    dimage_raw = unit_back(image_raw, image_inv, dimage)
    return (
        jnp.dot(text_pool.T, dtext_raw, precision=HIGHEST),
        jnp.dot(image_pool.T, dimage_raw, precision=HIGHEST),
        jnp.dot(dtext_raw, text_embed32.T, precision=HIGHEST),
        jnp.dot(dimage_raw, image_embed32.T, precision=HIGHEST),
    )


def pad_rows(x, rows):
    return jnp.pad(x, ((0, rows - x.shape[0]), (0, 0)))


def body(
    text,
    patches,
    cotangent,
    region_counts,
    phrase_starts,
    phrase_lengths,
    box_patches,
    query_weight,
    key_weight,
    value_weight,
    attn_out_weight,
    cross_query_weight,
    cross_key_weight,
    cross_value_weight,
    cross_out_weight,
    image_weight,
    ffn_in_weight,
    ffn_out_weight,
    text_embed_weight,
    image_embed_weight,
    *norm_shards,
):
    dp = lax.axis_size("dp")
    dims = split_dims(dp)
    mp = lax.axis_index("mp")
    half_pairs, patch_count, _ = patches.shape
    length, model_width = text.shape[1:]
    half = query_weight.shape[1]
    rows = query_weight.shape[0]
    hidden_blocks = ffn_in_weight.shape[1] // half
    embed_half = text_embed_weight.shape[1] // 2
    image_rows_own = image_weight.shape[0]

    def own_half(x, size, dim):
        return lax.dynamic_slice_in_dim(x, mp * size, size, dim)

    text, cotangent = own_half(text, half_pairs, 0), own_half(cotangent, half_pairs, 0)
    region_counts, phrase_starts = own_half(region_counts, half_pairs, 0), own_half(phrase_starts, half_pairs, 0)
    phrase_lengths, box_patches = own_half(phrase_lengths, half_pairs, 0), own_half(box_patches, half_pairs, 0)

    padded = -(-rows // 16) * 16
    small = jnp.concatenate(
        [own_half(text_embed_weight, embed_half, 1), own_half(image_embed_weight, embed_half, 1)]
        + [jnp.pad(jnp.stack(norm_shards, 1), ((0, 0), (0, half - 2 * embed_half - len(norm_shards))))],
        1,
    )
    ffn_out_t = ffn_out_weight.T
    shards = [
        own_half(image_weight, half, 1),
        query_weight,
        key_weight,
        value_weight,
        attn_out_weight.T,
        small,
        cross_key_weight,
        cross_value_weight,
        cross_query_weight,
        cross_out_weight.T,
        *(ffn_in_weight[:, k * half : (k + 1) * half] for k in range(hidden_blocks)),
        *(ffn_out_t[:, k * half : (k + 1) * half] for k in range(hidden_blocks)),
    ]
    real = [s.shape[0] for s in shards]
    shards = [pad_rows(s, -(-s.shape[0] // 16) * 16) for s in shards]
    gathered = gather(shards, dims)

    def merge(g, n):
        g = g.reshape(2, dp, *g.shape[-2:])[:, :, :n]
        return g.reshape(2, dp * n, g.shape[-1])

    gathered = [merge(g, n) for g, n in zip(gathered, real)]

    def columns(g):
        return jnp.concatenate([g[0], g[1]], 1)

    def blocks(gs):
        return jnp.concatenate([g[0] for g in gs] + [g[1] for g in gs], 1)

    image_w, query_w, key_w, value_w, attn_out_t = (columns(g) for g in gathered[:5])
    embeds = gathered[5]
    text_embed32 = columns(embeds[:, :, :embed_half]).astype(F32)
    image_embed32 = columns(embeds[:, :, embed_half : 2 * embed_half]).astype(F32)
    norms = embeds[0, :, 2 * embed_half : 2 * embed_half + len(norm_shards)].astype(F32).T
    gain_one, bias_one, gain_two, bias_two, gain_three, bias_three = (norms[k] for k in range(6))
    cross_key_w, cross_value_w, cross_query_w, cross_out_t = (columns(g) for g in gathered[6:10])
    ffn_in_w = blocks(gathered[10 : 10 + hidden_blocks])
    ffn_out_tw = blocks(gathered[10 + hidden_blocks :])

    text_rows = text.reshape(half_pairs * length, model_width)
    patch_rows = patches.reshape(half_pairs * patch_count, -1)
    image_rows = matmul(patch_rows, image_w).astype(BF16)
    image32 = image_rows.astype(F32).reshape(half_pairs, patch_count, model_width)
    queries = split_heads(matmul(text_rows, query_w).astype(BF16), half_pairs)
    key_heads = split_heads(matmul(text_rows, key_w).astype(BF16), half_pairs)
    value_heads = split_heads(matmul(text_rows, value_w).astype(BF16), half_pairs)
    self_mixed, self_total = attend(queries, key_heads, value_heads)
    first = text_rows.astype(F32) + contract_cols(self_mixed, attn_out_t)
    hidden_one, normed_one, inv_one = layer_norm(first, gain_one, bias_one)
    low_one = hidden_one.astype(BF16)
    cross_queries = split_heads(matmul(low_one, cross_query_w).astype(BF16), half_pairs)
    cross_keys = split_heads(matmul(image_rows, cross_key_w).astype(BF16), half_pairs)
    cross_values = split_heads(matmul(image_rows, cross_value_w).astype(BF16), half_pairs)
    cross_mixed, cross_total = attend(cross_queries, cross_keys, cross_values)
    second = hidden_one + contract_cols(cross_mixed, cross_out_t)
    hidden_two, normed_two, inv_two = layer_norm(second, gain_two, bias_two)
    low_two = hidden_two.astype(BF16)
    inner = matmul(low_two, ffn_in_w)
    active = jax.nn.gelu(inner, approximate=False).astype(BF16)
    third = hidden_two + contract_cols(active, ffn_out_tw)
    output, normed_three, inv_three = layer_norm(third, gain_three, bias_three)
    output3 = output.reshape(half_pairs, length, model_width)
    joined = output3.astype(BF16)

    text_pool = jnp.mean(text.astype(F32), 1)
    image_pool = jnp.mean(image32, 1)
    grad_text_embed, grad_image_embed, text_extra, image_pool_grad = contrast(
        text_pool, image_pool, text_embed32, image_embed32
    )
    text_extra = (text_extra / length)[:, None, :]
    image_pool_grad = image_pool_grad / patch_count
    positions = jnp.arange(length, dtype=jnp.int32)
    slots = jnp.arange(phrase_starts.shape[1], dtype=jnp.int32)
    valid = (slots[None, :] < region_counts[:, None]).astype(F32)
    ends = phrase_starts + phrase_lengths
    inside = ((positions >= phrase_starts[..., None]) & (positions < ends[..., None])).astype(F32) * valid[..., None]
    span_weight = inside / phrase_lengths[..., None].astype(F32)
    chosen = (
        jnp.sum((box_patches[..., None] == jnp.arange(patch_count, dtype=jnp.int32)).astype(F32), axis=2)
        / box_patches.shape[2]
    )
    phrase = jnp.einsum("pbt,ptd->pbd", span_weight, output3, precision=HIGHEST)
    region = jnp.einsum("pbn,pnd->pbd", chosen, image32, precision=HIGHEST)
    mismatch = (phrase - region) * valid[..., None]
    box_text = jnp.einsum("pbt,pbd->ptd", span_weight, mismatch, precision=HIGHEST)
    box_image = -jnp.einsum("pbn,pbd->pnd", chosen, mismatch, precision=HIGHEST)
    image_extra = (box_image + image_pool_grad[:, None, :]).reshape(-1, model_width)

    upstream = cotangent.astype(F32).reshape(-1, model_width) + box_text.reshape(-1, model_width)
    grad_third, gain_three_grad, bias_three_grad = norm_back(upstream, normed_three, inv_three, gain_three)
    low_third = grad_third.astype(BF16)
    grad_ffn_out_t = contract_rows(low_third, active)
    dactive = matmul(low_third, ffn_out_tw)
    gelu_pull = jax.vjp(lambda values: jax.nn.gelu(values, approximate=False), inner)[1]
    dinner = gelu_pull(dactive)[0].astype(BF16)
    grad_ffn_in = contract_rows(low_two, dinner)
    grad_second = grad_third + contract_cols(dinner, ffn_in_w)
    grad_second, gain_two_grad, bias_two_grad = norm_back(grad_second, normed_two, inv_two, gain_two)
    low_second = grad_second.astype(BF16)
    grad_cross_out_t = contract_rows(low_second, cross_mixed)
    dcross = split_heads(matmul(low_second, cross_out_t).astype(BF16), half_pairs)
    dqueries, dkeys, dvalues = attend_back(cross_queries, cross_keys, cross_values, cross_total, dcross)
    grad_cross_query = contract_rows(low_one, dqueries)
    grad_first = grad_second + contract_cols(dqueries, cross_query_w)
    grad_cross_key = contract_rows(image_rows, dkeys)
    grad_cross_value = contract_rows(image_rows, dvalues)
    dimage = contract_cols(dkeys, cross_key_w) + contract_cols(dvalues, cross_value_w) + image_extra
    low_image = dimage.astype(BF16)
    grad_image = contract_rows(patch_rows, low_image)
    patch_grad = contract_cols(low_image, image_w).reshape(patches.shape)
    grad_first, gain_one_grad, bias_one_grad = norm_back(grad_first, normed_one, inv_one, gain_one)
    low_first = grad_first.astype(BF16)
    grad_attn_out_t = contract_rows(low_first, self_mixed)
    dself = split_heads(matmul(low_first, attn_out_t).astype(BF16), half_pairs)
    dqueries, dkeys, dvalues = attend_back(queries, key_heads, value_heads, self_total, dself)
    grad_query = contract_rows(text_rows, dqueries)
    grad_key = contract_rows(text_rows, dkeys)
    grad_value = contract_rows(text_rows, dvalues)
    dtext = contract_cols(dqueries, query_w) + contract_cols(dkeys, key_w) + contract_cols(dvalues, value_w)
    text_grad = (grad_first + dtext).reshape(half_pairs, length, model_width) + text_extra

    def halves(g):
        g = g.astype(BF16)
        return jnp.stack([g[:, :half], g[:, half:]], 0)

    def hidden_halves(g):
        g = g.astype(BF16)
        return [
            jnp.stack([g[:, k * half : (k + 1) * half], g[:, (hidden_blocks + k) * half : (hidden_blocks + k + 1) * half]])
            for k in range(hidden_blocks)
        ]

    norm_grads = jnp.stack(
        [gain_one_grad, bias_one_grad, gain_two_grad, bias_two_grad, gain_three_grad, bias_three_grad], 1
    ).astype(BF16)
    norm_grads = jnp.pad(norm_grads, ((0, 0), (0, half - 2 * embed_half - len(norm_shards))))
    text_half, image_half = grad_text_embed.astype(BF16), grad_image_embed.astype(BF16)
    small_grads = jnp.stack(
        [
            jnp.concatenate(
                [text_half[:, k * embed_half : (k + 1) * embed_half], image_half[:, k * embed_half : (k + 1) * embed_half], norm_grads], 1
            )
            for k in range(2)
        ]
    )
    grads = [
        *hidden_halves(grad_ffn_out_t),
        *hidden_halves(grad_ffn_in),
        halves(grad_cross_out_t),
        halves(grad_cross_query),
        halves(grad_cross_key),
        halves(grad_cross_value),
        halves(grad_image),
        halves(grad_attn_out_t),
        halves(grad_query),
        halves(grad_key),
        halves(grad_value),
        small_grads,
    ]
    shared = (2 * hidden_blocks + 4, len(grads) - 1)

    def cut(g):
        n = g.shape[1] // dp
        g = g.reshape(2, dp, n, g.shape[-1])
        g = jnp.pad(g, ((0, 0), (0, 0), (0, -(-n // 16) * 16 - n), (0, 0)))
        return g.reshape(2, *dims, *g.shape[-2:])

    results = scatter([cut(g) for g in grads], shared, (joined, text_grad), dims)
    joined_all, text_grad_all = (r.reshape(2 * half_pairs, length, model_width) for r in results[len(grads) :])
    sums = [r[..., :n, :] for r, n in zip(results, [g.shape[1] // dp for g in grads])]
    ffn_out_own = jnp.concatenate(sums[:hidden_blocks], 1).T
    ffn_in_own = jnp.concatenate(sums[hidden_blocks : 2 * hidden_blocks], 1)
    cross_out_own, cross_query_own, cross_key_own, cross_value_own, image_own, attn_out_own, query_own, key_own, value_own, small_own = sums[2 * hidden_blocks :]
    own_norm = lax.dynamic_index_in_dim(small_own, mp, 0, keepdims=False)[:, 2 * embed_half :]
    return (
        joined_all,
        text_grad_all,
        patch_grad,
        query_own,
        key_own,
        value_own,
        attn_out_own.T,
        cross_query_own,
        cross_key_own,
        cross_value_own,
        cross_out_own.T,
        jnp.concatenate([image_own[0], image_own[1]], 1),
        ffn_in_own,
        ffn_out_own,
        jnp.concatenate([small_own[0, :, :embed_half], small_own[1, :, :embed_half]], 1),
        jnp.concatenate([small_own[0, :, embed_half : 2 * embed_half], small_own[1, :, embed_half : 2 * embed_half]], 1),
        own_norm[:, 0],
        own_norm[:, 1],
        own_norm[:, 2],
        own_norm[:, 3],
        own_norm[:, 4],
        own_norm[:, 5],
    )


def solution(mesh):
    pairs, weight, turned, single = P("dp", None, None), P("dp", "mp"), P("mp", "dp"), P("dp", None)
    weights = (weight, weight, weight, turned, weight, weight, weight, turned, single, weight, turned, single, single)
    norms = (P("dp"),) * 6
    halves = P(("dp", "mp"), None, None)
    in_specs = (pairs, halves, pairs, P("dp"), single, single, pairs) + weights + norms
    out_specs = (pairs, pairs, halves) + weights + norms
    return jax.shard_map(body, mesh=mesh, in_specs=in_specs, out_specs=out_specs, check_vma=False)
```

time: 1340 us -> 635 us (0.47)
  blocking collectives: 659 us -> 32.8 us
  Pallas kernels: 0 us -> 233 us
  waiting for transfers between devices: 215 us -> 0 us
  starting transfers between devices: 60.1 us -> 0 us
  local copies, waits for them, and re-layouts: 151 us -> 182 us
  matrix products: 152 us -> 127 us
  other arithmetic: 69 us -> 44.9 us
  between operations: 18.9 us -> 3.02 us
    all_gather x14 -> x1, blocking collectives: 546 us -> 32.8 us  [contrast(): everyone = lax.all_gather(both, ('dp', 'mp'), axis=0, tiled=True)]
    pallas_call x0 -> x2, Pallas kernels: none -> 233 us  [the longest x1 128 us: scatter(): pl.pallas_call(functools.partial(scatter_kernel, dims, count, shared, ext...]
    unnamed x2 -> x0, blocking collectives: 113 us -> none
    all_to_all x8 -> x0, waiting for transfers between devices: 93.1 us -> none  [sum_at_owner(): lax.all_to_all(parts, axis, split_axis=0, concat_axis=0, tiled=True)]
    all_gather x4 -> x0, waiting for transfers between devices: 87.9 us -> none  [the longest x1 48.7 us: gather_weights(): lax.all_gather(ffn_out_w, 'dp', axis=1, tiled=True)]
    all_to_all x8 -> x0, starting transfers between devices: 59.2 us -> none  [sum_at_owner(): lax.all_to_all(parts, axis, split_axis=0, concat_axis=0, tiled=True)]
    psum x6 -> x0, waiting for transfers between devices: 31.6 us -> none  [the longest x3 24.5 us: branch_sum(): return lax.psum(partial_sum, 'mp')]
    another operation x0 -> x18, other arithmetic: none -> 22.6 us  [the longest x9 10.6 us: halves(): return jnp.stack([g[:, :half], g[:, half:]], 0)]
  transfers between devices with their start and end apart: 19 -> 0, of which waited for: 10 -> 0; matrix products, arithmetic and copies ran while one was open for 17% -> 0% of each run, Pallas kernels for 0% -> 0%
where the time goes in v1:
time: 635 us; the launch traced here: 623 us
  Pallas kernels  233 us (37%)
  local copies, waits for them, and re-layouts  182 us (29%)
  matrix products  127 us (20%)
  other arithmetic  44.9 us (7%)
  blocking collectives  32.8 us (5%)
    pallas_call x1, Pallas kernels, scatter(): pl.pallas_call(functools.partial(scatter_kernel, dims, count, shared, ext...  128 us
    pallas_call x1, Pallas kernels, gather(): pl.pallas_call(functools.partial(gather_kernel, dims, count), out_shape=[...  105 us
    reshape x15, local copies, waits for them, and re-layouts, split_heads(): return flat.reshape(pair_count, -1, flat.shape[-1] // HEAD_DIM, HEAD_DIM)  46.5 us
    unnamed x366, local copies, waits for them, and re-layouts  40.5 us
    dot_general x11, matrix products, matmul(): return jnp.dot(left, right, preferred_element_type=F32)  35.8 us
    dot_general x12, matrix products, contract_cols(): lax.dot_general(left, right, (((1,), (1,)), ((), ())), preferred_element_...  33.2 us
    all_gather x1, blocking collectives, contrast(): everyone = lax.all_gather(both, ('dp', 'mp'), axis=0, tiled=True)  32.8 us
    dot_general x11, matrix products, contract_rows(): lax.dot_general(left, right, (((0,), (0,)), ((), ())), preferred_element_...  21.1 us

profile of v1, /device:TPU:12, one launch (start us, length us, event | category | flops | bytes accessed | tf_op | source)
XLA Modules:
  0.0 622.6 jit_solution(17463533852414559340)
XLA Ops:
  13.0 104.9 %gather_weights.1 = (bf16[2,4,2,2,64,384]{5,4,3,2,1,0:T(8,128)(2,1)}, bf16[2,4,2,2,48,384]{5,4,3,2,1,0:T(8,128)(2,1)}, bf16[2,4,2,2,48,384]{5,4,3,2,1,0:T(8,128)...) custom-call(bf16[64,384]{1,0:T(8,128)(2,1)} %constant_dynamic-slice_, ...), custom_call_target="tpu_custom_call" | custom-call | tf_op jit(solution)/shard_map/gather_weights/pallas_call | solution.py:231
  165.8 32.8 %all-gather = bf16[32,6,512]{2,1,0:T(8,128)(2,1)S(1)} all-gather(bf16[1,6,512]{2,1,0:T(8,128)(2,1)S(1)} %maximum_bitcast_fusion.1), channel_id=1, replica_groups=mesh['dp'=16,'mp'=2] {'dp','mp'}, dimensions={0}, use_global_device_ids=true | all-gather | bytes 202752 | tf_op jit(solution)/shard_map/all_gather | solution.py:394
  205.6 3.9 reshape.530
  209.4 6.2 %copy.219 = bf16[6,145,12,64]{1,3,2,0:T(8,128)(2,1)} copy(bf16[6,145,12,64]{3,2,1,0:T(8,128)(2,1)} %reshape.530) | data formatting | bytes 2672640 | tf_op jit(solution)/shard_map/reshape | solution.py:355
  215.7 3.9 reshape.531
  219.5 6.2 copy.218
  231.2 3.1 copy.213
  245.0 3.2 copy.228
  264.0 3.3 fusion.22
  275.5 14.7 %multiply_convert_fusion.2 = (bf16[366,3072]{1,0:T(8,128)(2,1)S(1)}, f32[366,3072]{1,0:T(8,128)}, f32[366,3072]{1,0:T(8,128)}) fusion(bf16[768,3072]{1,0:T(8,128)(2,1)} %copy-done.132, f32[366,768]{1,0:T(8,128)S(1)} %get-tuple-element.238, f32[768]{0:T(1024)S(1)} %copy-done.156, f32[768]{0:T(1024)S(1)} %copy-done.151, f32[366]{0:T(512)S(1)} %add_rsqrt_fusion.1, ...), kind=kOutput, calls=%fused_computation.11 | convolution fusion | flops 1801492992 | bytes 17095536 | tf_op jit(solution)/shard_map/dot_general | solution.py:329
  307.7 7.8 %add_convert_fusion = bf16[366,3072]{1,0:T(8,128)(2,1)S(1)} fusion(f32[366,3072]{1,0:T(8,128)} %get-tuple-element.129, f32[366,3072]{1,0:T(8,128)} %get-tuple-element.239, bf16[768,3072]{1,0:T(8,128)(2,1)} %copy-done.131, f32[366,768]{1,0:T(8,128)S(1)} %subtract_multiply_fusion.2), kind=kOutput, calls=%fused_computation.10 | convolution fusion | flops 1743026688 | bytes 17086464 | tf_op jit(solution)/shard_map/dot_general | solution.py:329
  324.8 3.4 copy.230
  328.2 4.8 convolution_convert_fusion
  348.8 3.3 copy.231
  352.2 5.5 reshape.516
  357.7 3.3 convolution_convert_fusion.13
  396.8 3.3 copy.229
  400.1 5.6 reshape.515
  405.7 3.2 convolution_convert_fusion.14
  437.7 3.1 convolution_add_fusion.2
  461.0 4.6 add_convert_fusion.1
  468.7 4.9 fusion.32
  473.6 4.5 reshape.526
  479.7 127.8 %scatter_gradients.1 = (f32[48,384]{1,0:T(8,128)}, f32[48,384]{1,0:T(8,128)}, f32[48,384]{1,0:T(8,128)}, f32[48,384]{1,0:T(8,128)}, f32[48,384]{1,0:T(8,128)}, /...) custom-call(bf16[2,4,2,2,48,384]{5,4,3,2,1,0:T(8,128)(2,1)} %pad_max, ...), custom_call_target="tpu_custom_call" | custom-call | tf_op jit(solution)/shard_map/scatter_gradients/pallas_call | solution.py:308
  (577 shorter events, 252.3 us)
Async XLA Ops:
  0.7 6.9 %copy-start = (bf16[64,768]{1,0:T(8,128)(2,1)S(1)}, bf16[64,768]{1,0:T(8,128)(2,1)}, u32[]{:S(2)}) copy-start(bf16[64,768]{1,0:T(8,128)(2,1)} %param.41) | copy-start | bytes 294916
  7.5 156.4 %copy-start.114 = (f32[6,6,145]{2,1,0:T(8,128)}, f32[6,6,145]{2,1,0:T(8,128)S(1)}, u32[]{:S(2)}) copy-start(f32[6,6,145]{2,1,0:T(8,128)S(1)} %convert_reduce_fusion.2) | copy-start | bytes 62644
  11.3 119.6 %copy-start.109 = (bf16[366,768]{1,0:T(8,128)(2,1)}, bf16[366,768]{1,0:T(8,128)(2,1)S(1)}, u32[]{:S(2)}) copy-start(bf16[366,768]{1,0:T(8,128)(2,1)S(1)} %reshape.501) | copy-start | bytes 1686532
  139.1 21.8 %copy-start.31 = (bf16[1,4,2,2,48,384]{5,4,3,2,1,0:T(8,128)(2,1)}, bf16[1,4,2,2,48,384]{5,4,3,2,1,0:T(8,128)(2,1)S(1)}, u32[]{:S(2)}) copy-start(bf16[1,4,2,2,48,384]{5,4,3,2,1,0:T(8,128)(2,1)S(1)} %get-tuple-element.192) | copy-start | bytes 1769476
  139.1 21.8 %copy-start.33 = (bf16[1,4,2,2,48,384]{5,4,3,2,1,0:T(8,128)(2,1)}, bf16[1,4,2,2,48,384]{5,4,3,2,1,0:T(8,128)(2,1)S(1)}, u32[]{:S(2)}) copy-start(bf16[1,4,2,2,48,384]{5,4,3,2,1,0:T(8,128)(2,1)S(1)} %get-tuple-element.193) | copy-start | bytes 1769476
  141.1 17.5 %copy-start.98 = (bf16[1,4,2,2,48,384]{5,4,3,2,1,0:T(8,128)(2,1)}, bf16[1,4,2,2,48,384]{5,4,3,2,1,0:T(8,128)(2,1)S(1)}, u32[]{:S(2)}) copy-start(bf16[1,4,2,2,48,384]{5,4,3,2,1,0:T(8,128)(2,1)S(1)} %get-tuple-element.180) | copy-start | bytes 1769476
  141.1 17.5 %copy-start.100 = (bf16[1,4,2,2,48,384]{5,4,3,2,1,0:T(8,128)(2,1)}, bf16[1,4,2,2,48,384]{5,4,3,2,1,0:T(8,128)(2,1)S(1)}, u32[]{:S(2)}) copy-start(bf16[1,4,2,2,48,384]{5,4,3,2,1,0:T(8,128)(2,1)S(1)} %get-tuple-element.181) | copy-start | bytes 1769476
  165.3 34.1 %copy-start.142 = (f32[6,256]{1,0:T(8,128)S(1)}, f32[6,256]{1,0:T(8,128)}, u32[]{:S(2)}) copy-start(f32[6,256]{1,0:T(8,128)} %copy-done.141) | copy-start | bytes 18436
  165.8 35.4 %copy-start.118 = (bf16[768,128]{1,0:T(8,128)(2,1)S(1)}, bf16[768,128]{1,0:T(8,128)(2,1)}, u32[]{:S(2)}) copy-start(bf16[768,128]{1,0:T(8,128)(2,1)} %copy-done.117) | copy-start | bytes 589828
  165.8 35.3 %copy-start.120 = (bf16[768,128]{1,0:T(8,128)(2,1)S(1)}, bf16[768,128]{1,0:T(8,128)(2,1)}, u32[]{:S(2)}) copy-start(bf16[768,128]{1,0:T(8,128)(2,1)} %copy-done.119) | copy-start | bytes 589828
  165.8 35.3 %copy-start.157 = (f32[6]{0:T(128)S(1)}, f32[6]{0:T(128)}, u32[]{:S(2)}) copy-start(f32[6]{0:T(128)} %get-tuple-element.225) | copy-start | bytes 76
  165.8 35.3 %copy-start.158 = (f32[6]{0:T(128)S(1)}, f32[6]{0:T(128)}, u32[]{:S(2)}) copy-start(f32[6]{0:T(128)} %get-tuple-element.226) | copy-start | bytes 76
  240.7 31.9 %copy-start.152 = (f32[366]{0:T(512)}, f32[366]{0:T(512)S(1)}, u32[]{:S(2)}) copy-start(f32[366]{0:T(512)S(1)} %add_rsqrt_fusion.2) | copy-start | bytes 4396
  264.0 83.1 %copy-start.87 = (f32[6,12,61]{2,1,0:T(8,128)}, f32[6,12,61]{2,1,0:T(8,128)S(1)}, u32[]{:S(2)}) copy-start(f32[6,12,61]{2,1,0:T(8,128)S(1)} %log_add_fusion.1) | copy-start | bytes 52708
  272.6 17.6 %slice-start.4 = ((s8[4718592]{0:T(1024)(128)(4,1)}), s8[4194304]{0:T(1024)(128)(4,1)S(1)}, s32[]{:S(2)}) async-start(s8[4718592]{0:T(1024)(128)(4,1)} %bitcast.296), calls=%async_computation.4 | async-start | bytes 8388608
  275.1 15.0 %copy-start.26 = (f32[366,768]{1,0:T(8,128)}, f32[366,768]{1,0:T(8,128)S(1)}, u32[]{:S(2)}) copy-start(f32[366,768]{1,0:T(8,128)S(1)} %get-tuple-element.238) | copy-start | bytes 3373060
  275.5 14.8 %slice-start.5 = ((s8[4718592]{0:T(1024)(128)(4,1)}), s8[524288]{0:T(1024)(128)(4,1)S(1)}, s32[]{:S(2)}) async-start(s8[4718592]{0:T(1024)(128)(4,1)} %bitcast.296), calls=%async_computation.5 | async-start | bytes 1048576
  307.3 8.2 %slice-start.6 = ((s8[4718592]{0:T(1024)(128)(4,1)}), s8[4194304]{0:T(1024)(128)(4,1)S(1)}, s32[]{:S(2)}) async-start(s8[4718592]{0:T(1024)(128)(4,1)} %bitcast.298), calls=%async_computation.6 | async-start | bytes 8388608
  307.7 7.9 %copy-start.84 = (f32[366,768]{1,0:T(8,128)}, f32[366,768]{1,0:T(8,128)S(1)}, u32[]{:S(2)}) copy-start(f32[366,768]{1,0:T(8,128)S(1)} %subtract_multiply_fusion.2) | copy-start | bytes 3373060
  307.7 7.9 %copy-start.27 = (f32[366,768]{1,0:T(8,128)S(1)}, f32[366,768]{1,0:T(8,128)}, u32[]{:S(2)}) copy-start(f32[366,768]{1,0:T(8,128)} %copy-done.26) | copy-start | bytes 3373060
  307.7 7.9 %slice-start.7 = ((s8[4718592]{0:T(1024)(128)(4,1)}), s8[524288]{0:T(1024)(128)(4,1)S(1)}, s32[]{:S(2)}) async-start(s8[4718592]{0:T(1024)(128)(4,1)} %bitcast.298), calls=%async_computation.7 | async-start | bytes 1048576
  352.2 10.1 %slice-start.2 = ((s8[4718592]{0:T(1024)(128)(4,1)}), s8[524288]{0:T(1024)(128)(4,1)S(1)}, s32[]{:S(2)}) async-start(s8[4718592]{0:T(1024)(128)(4,1)} %bitcast.200), calls=%async_computation.2 | async-start | bytes 1048576
  607.6 7.0 %copy-start.82 = (bf16[2,6,61,768]{3,2,1,0:T(8,128)(2,1)S(1)}, bf16[2,6,61,768]{3,2,1,0:T(8,128)(2,1)}, u32[]{:S(2)}) copy-start(bf16[2,6,61,768]{3,2,1,0:T(8,128)(2,1)} %get-tuple-element.78) | copy-start | bytes 3373060
  615.8 6.5 %copy-start.1 = (bf16[64,768]{1,0:T(8,128)(2,1)S(1)}, bf16[64,768]{1,0:T(8,128)(2,1)}, u32[]{:S(2)}) copy-start(bf16[64,768]{1,0:T(8,128)(2,1)} %param.41) | copy-start | bytes 294916
  (146 other events, 349.1 us)
